TPU v7x, 32 devices: a whole 2x2x4 slice. The times are simulated.
32 devices in a mesh: section: 4 (over y, x), ctx: 8 (over z, core).
Axes of the slice: x: 2, y: 2, z: 4, core: 2. Of those that a mesh axis runs over, the one named last changes fastest.
Arguments:
- queries: bfloat16 [2, 4, 1024, 1024], P(None, 'section', 'ctx'), may hold values from -8 to 8
- out_grad: bfloat16 [2, 4, 1024, 1024], P(None, 'section', 'ctx'), may hold values from -6 to 6
- keys: bfloat16 [4, 1024, 128], P('section', 'ctx'), may hold values from -4 to 4
- values: bfloat16 [4, 1024, 128], P('section', 'ctx'), may hold values from -6 to 6
- entering_keys: bfloat16 [1024, 128], P('ctx'), may hold values from -4 to 4
- entering_values: bfloat16 [1024, 128], P('ctx'), may hold values from -6 to 6
- key_grads_in: float32 [4, 1024, 128], P('section', 'ctx'), may hold values from -4 to 4
- value_grads_in: float32 [4, 1024, 128], P('section', 'ctx'), may hold values from -4 to 4
- group_order: int32 [8], replicated, may hold values from 0 to 7, each once
Outputs:
- query_grads: bfloat16 [2, 4, 1024, 1024], P(None, 'section', 'ctx')
- key_grads: float32 [2, 4, 1024, 128], P(None, 'section', 'ctx')
- value_grads: float32 [2, 4, 1024, 128], P(None, 'section', 'ctx')
Inputs may be any that keep to these rules, and one draw needn't show every extreme that they name: `group_order`: each number 0 to 7 appears once.
All inputs are finite; a program needn't handle non-finite values.
Results may differ from a plain program's by a relative error of at most 0.0062.
Values may be sent and summed in bfloat16 or wider, within the bound.
No kernel may reach another device: no remote copies, remote signals or barrier semaphores. Data moves between devices by JAX's collectives and lax.ppermute only.
A program may use at most 128 MiB of HBM per device.

v0:
```python
import math

import jax
import jax.numpy as jnp
from jax import lax
from jax.sharding import PartitionSpec as P

HEADS = 8


MASK_FILL = -1e30


def shifted(block, axis, distance):
    devices = range(lax.axis_size(axis))
    route = [(i - distance, i) for i in devices if i - distance in devices]
    return lax.ppermute(block, axis, route)


def body(
    queries,
    out_grad,
    keys,
    values,
    entering_keys,
    entering_values,
    key_grads_in,
    value_grads_in,
    group_order,
):
    local_rows = keys.shape[1]
    head_dim = keys.shape[2]
    ctx_count = lax.axis_size("ctx")
    whole_len = local_rows * ctx_count
    score_scale = 1.0 / math.sqrt(head_dim)
    ctx_index = lax.axis_index("ctx")
    slot_ids = jnp.arange(ctx_count, dtype=jnp.int32)
    own_group = jnp.sum(jnp.where(slot_ids == ctx_index, group_order, 0))
    query_pos = own_group * local_rows + jnp.arange(local_rows, dtype=jnp.int32)
    query_rows = jnp.repeat(query_pos, HEADS)
    flat_rows = local_rows * HEADS

    def key_positions(row_count):
        row_ids = jnp.arange(row_count, dtype=jnp.int32)
        shard_ids = row_ids // local_rows
        group_ids = jnp.sum(
            jnp.where(shard_ids[:, None] == slot_ids[None, :], group_order[None, :], 0), axis=1
        )
        return group_ids * local_rows + row_ids % local_rows

    def one_tick(query_block, grad_block, kv_pair, carried):
        queries_flat = query_block.reshape(flat_rows, head_dim)
        grads_flat = grad_block.reshape(flat_rows, head_dim)

        def mask_for(row_count):
            return key_positions(row_count)[None, :] <= query_rows[:, None]

        def masked_scores(kv_piece, allowed):
            raw = (
                jnp.dot(queries_flat, kv_piece[:, :head_dim].T, preferred_element_type=jnp.float32)
                * score_scale
            )
            return jnp.where(allowed, raw, MASK_FILL)

        start_stats = (
            jnp.full((flat_rows,), MASK_FILL, jnp.float32),
            jnp.zeros((flat_rows,), jnp.float32),
            jnp.zeros((flat_rows,), jnp.float32),
        )
        kv_piece = lax.all_gather(kv_pair, "ctx", axis=0, tiled=True)
        allowed = mask_for(kv_piece.shape[0])

        def row_update(state):
            biggest, totals, weighted = state
            scores = masked_scores(kv_piece, allowed)
            new_biggest = jnp.maximum(biggest, jnp.max(scores, axis=1))
            expo = jnp.where(allowed, jnp.exp(scores - new_biggest[:, None]), 0.0)
            prob_grads = jnp.dot(
                grads_flat, kv_piece[:, head_dim:].T, preferred_element_type=jnp.float32
            )
            new_totals = jnp.sum(expo, axis=1)
            new_weighted = jnp.sum(expo * prob_grads, axis=1)
            return (new_biggest, new_totals, new_weighted)

        def row_skipped(state):
            return state

        biggest, totals, weighted = lax.cond(jnp.any(allowed), row_update, row_skipped, start_stats)
        deltas = weighted / totals

        def piece_probs(kv_piece, allowed):
            scores = masked_scores(kv_piece, allowed)
            return jnp.where(allowed, jnp.exp(scores - biggest[:, None]), 0.0) / totals[:, None]

        start_grads = (
            jnp.zeros((flat_rows, head_dim), jnp.float32),
            jnp.zeros((whole_len, 2 * head_dim), jnp.float32),
        )
        grad_kv_piece = lax.all_gather(kv_pair, "ctx", axis=0, tiled=True)
        row_count = grad_kv_piece.shape[0]
        grad_allowed = mask_for(row_count)

        def grad_update(state):
            probs = piece_probs(grad_kv_piece, grad_allowed)
            prob_grads = jnp.dot(
                grads_flat, grad_kv_piece[:, head_dim:].T, preferred_element_type=jnp.float32
            )
            score_grad = (probs * (prob_grads - deltas[:, None])).astype(jnp.bfloat16)
            probs_half = probs.astype(jnp.bfloat16)
            query_acc = jnp.dot(
                score_grad, grad_kv_piece[:, :head_dim], preferred_element_type=jnp.float32
            )
            key_terms = (
                jnp.dot(score_grad.T, queries_flat, preferred_element_type=jnp.float32)
                * score_scale
            )
            value_terms = jnp.dot(probs_half.T, grads_flat, preferred_element_type=jnp.float32)
            new_rows = jnp.concatenate([key_terms, value_terms], axis=1)
            return (query_acc, new_rows)

        def grad_skipped(state):
            return state

        query_sum, terms = lax.cond(jnp.any(grad_allowed), grad_update, grad_skipped, start_grads)
        query_grad = (
            (query_sum * score_scale).astype(jnp.bfloat16).reshape(local_rows, HEADS * head_dim)
        )
        summed = lax.psum_scatter(terms, "ctx", scatter_dimension=0, tiled=True)
        return (query_grad, carried + summed)

    first_pair = jnp.concatenate([keys[0], values[0]], axis=1)
    first_carried = jnp.concatenate([key_grads_in[0], value_grads_in[0]], axis=1)
    first_query, first_acc = one_tick(queries[0, 0], out_grad[0, 0], first_pair, first_carried)
    moved_pair = shifted(first_pair, "section", -1)
    moved_acc = shifted(first_acc, "section", -1)
    is_last = lax.axis_index("section") == lax.axis_size("section") - 1
    entering_pair = jnp.concatenate([entering_keys, entering_values], axis=1)
    second_pair = jnp.where(is_last, entering_pair, moved_pair)
    second_query, second_acc = one_tick(queries[1, 0], out_grad[1, 0], second_pair, moved_acc)
    query_grads = jnp.stack([first_query, second_query], axis=0)[:, None]
    key_grads = jnp.stack([first_acc[:, :head_dim], second_acc[:, :head_dim]], axis=0)[:, None]
    value_grads = jnp.stack([first_acc[:, head_dim:], second_acc[:, head_dim:]], axis=0)[:, None]
    return (query_grads, key_grads, value_grads)


def solution(mesh):
    return jax.shard_map(
        body,
        mesh=mesh,
        in_specs=(
            P(None, "section", "ctx", None),
            P(None, "section", "ctx", None),
            P("section", "ctx", None),
            P("section", "ctx", None),
            P("ctx", None),
            P("ctx", None),
            P("section", "ctx", None),
            P("section", "ctx", None),
            P(),
        ),
        out_specs=(
            P(None, "section", "ctx", None),
            P(None, "section", "ctx", None),
            P(None, "section", "ctx", None),
        ),
        check_vma=False,
    )
```

profile of v0, /device:TPU:0, one launch (start us, length us, event | category | flops | bytes accessed | tf_op | source)
XLA Modules:
  0.0 124.9 jit_solution(15625753238397030192)
XLA Ops:
  7.2 1.3 %fusion.30 = s32[]{:T(128)} fusion(s32[8]{0:T(128)} %param.25, s32[]{:T(128)S(6)} %axis_index.22), kind=kLoop, calls=%fused_computation.66 | loop fusion | flops 23 | bytes 40 | tf_op jit(solution)/shard_map/reduce_sum | solution.py:38
  11.2 1.8 %fusion.32 = (bf16[1,1,128,1024]{3,2,1,0:T(8,128)(2,1)S(1)}, bf16[1,1,128,1024]{3,2,1,0:T(8,128)(2,1)}) fusion(bf16[2,1,128,1024]{3,2,1,0:T(8,128)(2,1)} %param.18), kind=kLoop, calls=%fused_computation.69 | loop fusion | bytes 1048576 | tf_op jit(solution)/shard_map/slice | solution.py:133
  13.0 1.8 %broadcast_compare_fusion = (pred[1024,1024]{1,0:T(32,128)(4,1)S(1)}, pred[]{:T(512)}) fusion(s32[1024]{0:T(1024)S(1)} %fusion.28, s32[1024]{0:T(1024)S(1)} %le.9), kind=kLoop, calls=%fused_computation.38 | loop fusion | flops 2097151 | bytes 1056769 | tf_op jit(solution)/shard_map/le | solution.py:56
  15.7 16.6 %all_gather.8 = bf16[1024,256]{1,0:T(8,128)(2,1)S(1)} all-gather(bf16[128,256]{1,0:T(8,128)(2,1)S(1)} %pad_maximum_fusion.2), channel_id=1, replica_groups=mesh['section'=4,'ctx'=8] {'ctx'}, dimensions={0}, use_global_device_ids=true | all-gather | bytes 589824 | tf_op jit(solution)/shard_map/all_gather | solution.py:99
  32.3 6.8 %conditional.4 = (f32[1024]{0:T(1024)}, f32[1024]{0:T(1024)S(1)}, f32[1024]{0:T(1024)S(1)}) conditional(s32[]{:T(128)} %convert_element_type.28, () %tuple.45, (bf16[1024,256]{1,0:T(8,128)(2,1)S(1)}, bf16[1024,128]{1,0:T(8,128)(2,1)S(1)}, pred[1024,1024]{1,0:T(32,128)(4,1)S(1)}, bf16[1024,128]{1,0:T(8,128)(2,1)S(1)}) %tuple.46), branch_computations={%region_3.4_spmd, %region_4.8_spmd} | conditional | flops 551548928 | bytes 18903064 | solution.py:88
  32.3 1.2 copy.20
  34.9 2.2 %multiply_reduce_fusion = f32[1024]{0:T(1024)S(1)} fusion(pred[1024,1024]{0,1:T(32,128)(4,1)S(1)} %copy.20, f32[1024,1024]{0,1:T(8,128)S(1)} %get-tuple-element.148, bf16[1024,128]{1,0:T(8,128)(2,1)S(1)} %get-tuple-element.81, f32[1024]{0:T(1024)} %broadcast_maximum_fusion, bf16[1024,256]{1,0:T(8,128)(2,1)S(1)} %get-tuple-element.80), kind=kOutput, calls=%fused_computation | convolution fusion | flops 274725888 | bytes 5775360 | tf_op jit(solution)/shard_map/cond/branch_1_fun/dot_general | solution.py:78
  37.1 1.9 %fusion.1 = f32[1024]{0:T(1024)S(1)} fusion(pred[1024,1024]{0,1:T(32,128)(4,1)S(1)} %copy.20, f32[1024,1024]{0,1:T(8,128)S(1)} %get-tuple-element.148, f32[1024]{0:T(1024)} %broadcast_maximum_fusion), kind=kLoop, calls=%fused_computation.4 | loop fusion | flops 5241856 | bytes 5251072 | tf_op jit(solution)/shard_map/cond/branch_1_fun/reduce_sum | solution.py:81
  39.0 5.5 %conditional.5 = (f32[1024,128]{1,0:T(8,128)}, f32[1024,256]{0,1:T(8,128)S(1)}) conditional(s32[]{:T(128)} %convert_element_type.28, () %tuple.44, (bf16[1024,256]{1,0:T(8,128)(2,1)S(1)}, bf16[1024,128]{1,0:T(8,128)(2,1)S(1)}, pred[1024,1024]{1,0:T(32,128)(4,1)S(1)}, f32[1024]{0:T(1024)}, f32[1024]{0:T(1024)S(1)}, ...), branch_computations={%region_8.9_spmd, %region_9.10_spmd} | conditional | flops 1352008704 | bytes 25452560 | solution.py:124
  39.1 2.2 %select_divide_fusion = f32[1024,1024]{1,0:T(8,128)S(1)} fusion(pred[1024,1024]{1,0:T(32,128)(4,1)S(1)} %get-tuple-element.82, bf16[1024,128]{1,0:T(8,128)(2,1)S(1)} %get-tuple-element.83, f32[1024]{0:T(1024)S(1)} %get-tuple-element.86, f32[1024]{0:T(1024)} %get-tuple-element.85, bf16[1024,256]{1,0:T(8,128)(2,1)S(1)} %get-tuple-element.84), kind=kOutput, calls=%fused_computation.10 | convolution fusion | flops 273678336 | bytes 5775360 | tf_op jit(solution)/shard_map/cond/branch_1_fun/dot_general | solution.py:60
  43.1 1.5 %fusion.8 = f32[1024,128]{1,0:T(8,128)} fusion(bf16[1024,1024]{1,0:T(8,128)(2,1)S(1)} %multiply_convert_fusion, bf16[1024,256]{1,0:T(8,128)(2,1)S(1)} %get-tuple-element.84), kind=kOutput, calls=%fused_computation.16 | convolution fusion | flops 268435456 | bytes 2883584 | tf_op jit(solution)/shard_map/cond/branch_1_fun/dot_general | solution.py:110
  44.6 1.3 %copy.22 = f32[1024,256]{1,0:T(8,128)} copy(f32[1024,256]{0,1:T(8,128)S(1)} %get-tuple-element.121) | data formatting | bytes 2097152 | tf_op jit(solution)/shard_map/cond | solution.py:124
  46.0 1.3 %collective-permute-start = (bf16[128,256]{1,0:T(8,128)(2,1)S(1)}, bf16[128,256]{1,0:T(8,128)(2,1)S(1)}, u32[]{:S(2)}, u32[]{:S(2)}) collective-permute-start(bf16[128,256]{1,0:T(8,128)(2,1)S(1)} %pad_maximum_fusion.2), channel_id=1, source_target_pairs={{8,0},{16,8},{24,16},{9,1},{17,9},{25,17},{10,2},{18,10},{26,18},{... | collective-permute-start | bytes 196616 | tf_op jit(solution)/shard_map/ppermute | solution.py:17
  48.5 3.7 %collective-permute-done = bf16[128,256]{1,0:T(8,128)(2,1)S(1)} collective-permute-done((bf16[128,256]{1,0:T(8,128)(2,1)S(1)}, bf16[128,256]{1,0:T(8,128)(2,1)S(1)}, u32[]{:S(2)}, u32[]{:S(2)}) %collective-permute-start) | collective-permute-done | bytes 65568 | tf_op jit(solution)/shard_map/ppermute | solution.py:17
  52.2 16.8 %all_gather.9 = bf16[1024,256]{1,0:T(8,128)(2,1)S(1)} all-gather(bf16[128,256]{1,0:T(8,128)(2,1)S(1)} %maximum_select_fusion), channel_id=1, replica_groups=mesh['section'=4,'ctx'=8] {'ctx'}, dimensions={0}, use_global_device_ids=true | all-gather | bytes 589824 | tf_op jit(solution)/shard_map/all_gather | solution.py:99
  69.0 6.8 %conditional.6 = (f32[1024]{0:T(1024)}, f32[1024]{0:T(1024)S(1)}, f32[1024]{0:T(1024)S(1)}) conditional(s32[]{:T(128)} %convert_element_type.28, () %tuple.49, (bf16[1024,256]{1,0:T(8,128)(2,1)S(1)}, bf16[1024,128]{1,0:T(8,128)(2,1)S(1)}, pred[1024,1024]{1,0:T(32,128)(4,1)S(1)}, bf16[1024,128]{1,0:T(8,128)(2,1)S(1)}) %tuple.50), branch_computations={%region_10.11_spmd, %region_11.15_spmd} | conditional | flops 551548928 | bytes 18903064 | solution.py:88
  71.6 2.2 %multiply_reduce_fusion.1 = f32[1024]{0:T(1024)S(1)} fusion(pred[1024,1024]{0,1:T(32,128)(4,1)S(1)} %copy.21, f32[1024,1024]{0,1:T(8,128)S(1)} %get-tuple-element.150, bf16[1024,128]{1,0:T(8,128)(2,1)S(1)} %get-tuple-element.92, f32[1024]{0:T(1024)} %broadcast_maximum_fusion.1, bf16[1024,256]{1,0:T(8,128)(2,1)S(1)} %get-tuple-element.91), kind=kOutput, calls=%fused_computation.19 | convolution fusion | flops 274725888 | bytes 5775360 | tf_op jit(solution)/shard_map/cond/branch_1_fun/dot_general | solution.py:78
  73.9 1.9 %fusion.12 = f32[1024]{0:T(1024)S(1)} fusion(pred[1024,1024]{0,1:T(32,128)(4,1)S(1)} %copy.21, f32[1024,1024]{0,1:T(8,128)S(1)} %get-tuple-element.150, f32[1024]{0:T(1024)} %broadcast_maximum_fusion.1), kind=kLoop, calls=%fused_computation.23 | loop fusion | flops 5241856 | bytes 5251072 | tf_op jit(solution)/shard_map/cond/branch_1_fun/reduce_sum | solution.py:81
  75.8 5.6 %conditional.7 = (f32[1024,128]{1,0:T(8,128)}, f32[1024,256]{0,1:T(8,128)S(1)}) conditional(s32[]{:T(128)} %convert_element_type.28, () %tuple.48, (bf16[1024,256]{1,0:T(8,128)(2,1)S(1)}, bf16[1024,128]{1,0:T(8,128)(2,1)S(1)}, pred[1024,1024]{1,0:T(32,128)(4,1)S(1)}, f32[1024]{0:T(1024)}, f32[1024]{0:T(1024)S(1)}, ...), branch_computations={%region_15.16_spmd, %region_16.17_spmd} | conditional | flops 1352008704 | bytes 25452560 | solution.py:124
  75.8 2.2 %select_divide_fusion.1 = f32[1024,1024]{1,0:T(8,128)S(1)} fusion(pred[1024,1024]{1,0:T(32,128)(4,1)S(1)} %get-tuple-element.93, bf16[1024,128]{1,0:T(8,128)(2,1)S(1)} %get-tuple-element.94, f32[1024]{0:T(1024)S(1)} %get-tuple-element.97, f32[1024]{0:T(1024)} %get-tuple-element.96, bf16[1024,256]{1,0:T(8,128)(2,1)S(1)} %get-tuple-element.95), kind=kOutput, calls=%fused_computation.29 | convolution fusion | flops 273678336 | bytes 5775360 | tf_op jit(solution)/shard_map/cond/branch_1_fun/dot_general | solution.py:60
  79.8 1.5 %fusion.19 = f32[1024,128]{1,0:T(8,128)} fusion(bf16[1024,1024]{1,0:T(8,128)(2,1)S(1)} %multiply_convert_fusion.1, bf16[1024,256]{1,0:T(8,128)(2,1)S(1)} %get-tuple-element.95), kind=kOutput, calls=%fused_computation.35 | convolution fusion | flops 268435456 | bytes 2883584 | tf_op jit(solution)/shard_map/cond/branch_1_fun/dot_general | solution.py:110
  81.3 1.4 %copy.23 = f32[1024,256]{1,0:T(8,128)} copy(f32[1024,256]{0,1:T(8,128)S(1)} %get-tuple-element.122) | data formatting | bytes 2097152 | tf_op jit(solution)/shard_map/cond | solution.py:124
  86.9 1.3 %collective-permute-start.1 = (f32[128,256]{1,0:T(8,128)S(1)}, f32[128,256]{1,0:T(8,128)S(1)}, u32[]{:S(2)}, u32[]{:S(2)}) collective-permute-start(f32[128,256]{1,0:T(8,128)S(1)} %maximum_add_fusion), channel_id=1, source_target_pairs={{8,0},{16,8},{24,16},{9,1},{17,9},{25,17},{10,2},{18,10},{26,18},{... | collective-permute-start | bytes 393224 | tf_op jit(solution)/shard_map/ppermute | solution.py:17
  88.3 28.2 %reduce-scatter.5.cloned.1.call-done = f32[128,256]{1,0:T(8,128)} async-done(((f32[1024,256]{1,0:T(8,128)}), f32[128,256]{1,0:T(8,128)}) %reduce-scatter.5.cloned.1.call-update) | async-done | bytes 131088 | tf_op jit(solution)/shard_map/reduce_scatter | solution.py:128
  (56 shorter events, 17.1 us)
Async XLA Ops:
  7.2 8.5 %copy-start.3 = (bf16[1,128,128]{2,1,0:T(8,128)(2,1)S(1)}, bf16[1,128,128]{2,1,0:T(8,128)(2,1)}, u32[]{:S(2)}) copy-start(bf16[1,128,128]{2,1,0:T(8,128)(2,1)} %param.19) | copy-start | bytes 98308
  7.2 8.5 %copy-start.2 = (bf16[1,128,128]{2,1,0:T(8,128)(2,1)S(1)}, bf16[1,128,128]{2,1,0:T(8,128)(2,1)}, u32[]{:S(2)}) copy-start(bf16[1,128,128]{2,1,0:T(8,128)(2,1)} %param.20) | copy-start | bytes 98308
  7.2 78.8 %reduce-scatter.3.cloned.1.call-start = ((), (), s32[]{:S(2)}) async-start(), calls=%async_computation.2 | async-start | bytes 1179648 | tf_op jit(solution)/shard_map/reduce_scatter | solution.py:128
  44.6 7.6 %copy-start.4 = (bf16[128,128]{1,0:T(8,128)(2,1)S(1)}, bf16[128,128]{1,0:T(8,128)(2,1)}, u32[]{:S(2)}) copy-start(bf16[128,128]{1,0:T(8,128)(2,1)} %param.22) | copy-start | bytes 98308
  44.6 7.6 %copy-start.5 = (bf16[128,128]{1,0:T(8,128)(2,1)S(1)}, bf16[128,128]{1,0:T(8,128)(2,1)}, u32[]{:S(2)}) copy-start(bf16[128,128]{1,0:T(8,128)(2,1)} %param.21) | copy-start | bytes 98308
  45.9 70.5 %reduce-scatter.5.cloned.1.call-start = ((), (), s32[]{:S(2)}) async-start(), calls=%async_computation.3 | async-start | bytes 1179648 | tf_op jit(solution)/shard_map/reduce_scatter | solution.py:128
  46.0 6.2 %collective-permute-start = (bf16[128,256]{1,0:T(8,128)(2,1)S(1)}, bf16[128,256]{1,0:T(8,128)(2,1)S(1)}, u32[]{:S(2)}, u32[]{:S(2)}) collective-permute-start(bf16[128,256]{1,0:T(8,128)(2,1)S(1)} %pad_maximum_fusion.2), channel_id=1, source_target_pairs={{8,0},{16,8},{24,16},{9,1},{17,9},{25,17},{10,2},{18,10},{26,18},{... | collective-permute-start | bytes 196616 | tf_op jit(solution)/shard_map/ppermute | solution.py:17
  81.3 4.7 %copy-start = (f32[1,128,128]{2,1,0:T(8,128)S(1)}, f32[1,128,128]{2,1,0:T(8,128)}, u32[]{:S(2)}) copy-start(f32[1,128,128]{2,1,0:T(8,128)} %param.24) | copy-start | bytes 196612
  81.3 4.7 %copy-start.1 = (f32[1,128,128]{2,1,0:T(8,128)S(1)}, f32[1,128,128]{2,1,0:T(8,128)}, u32[]{:S(2)}) copy-start(f32[1,128,128]{2,1,0:T(8,128)} %param.23) | copy-start | bytes 196612
  86.9 29.5 %collective-permute-start.1 = (f32[128,256]{1,0:T(8,128)S(1)}, f32[128,256]{1,0:T(8,128)S(1)}, u32[]{:S(2)}, u32[]{:S(2)}) collective-permute-start(f32[128,256]{1,0:T(8,128)S(1)} %maximum_add_fusion), channel_id=1, source_target_pairs={{8,0},{16,8},{24,16},{9,1},{17,9},{25,17},{10,2},{18,10},{26,18},{... | collective-permute-start | bytes 393224 | tf_op jit(solution)/shard_map/ppermute | solution.py:17
Sparse Core Ops, SparseCore 0:
  46.1 34.3 reduce-scatter.2
  82.9 33.5 reduce-scatter.4
where the time goes:
time: 126 us; the launch traced here: 125 us
  blocking collectives  33.3 us (26%)
  waiting for transfers between devices  31.9 us (25%)
  matrix products  16.9 us (13%)
  between operations  15.5 us (12%)
  other arithmetic  14.6 us (12%)
  local copies, waits for them, and re-layouts  9.7 us (8%)
  starting transfers between devices  2.66 us (2%)
    all_gather x2, blocking collectives, one_tick(): grad_kv_piece = lax.all_gather(kv_pair, 'ctx', axis=0, tiled=True)  33.3 us
    reduce_scatter x2, waiting for transfers between devices, one_tick(): summed = lax.psum_scatter(terms, 'ctx', scatter_dimension=0, tiled=True)  28.2 us
    dot_general x4, matrix products, masked_scores(): jnp.dot(queries_flat, kv_piece[:, :head_dim].T, preferred_element_type=jn...  6.07 us
    dot_general x2, matrix products, row_update(): jnp.dot(grads_flat, kv_piece[:, head_dim:].T, preferred_element_type=jnp....  4.4 us
    reduce_sum x2, other arithmetic, row_update(): new_totals = jnp.sum(expo, axis=1)  3.84 us
    ppermute x2, waiting for transfers between devices, shifted(): return lax.ppermute(block, axis, route)  3.73 us
    dot_general x2, matrix products, grad_update(): jnp.dot(score_grad, grad_kv_piece[:, :head_dim], preferred_element_type=j...  3.03 us
    cond x2, local copies, waits for them, and re-layouts, one_tick(): lax.cond(jnp.any(grad_allowed), grad_update, grad_skipped, start_grads)  2.7 us
  transfers between devices with their start and end apart: 4, of which 2 were waited for; matrix products, arithmetic and copies ran while one was open for 15% of the time, Pallas kernels for 0%

commit v1 on v0

v1 whole, which is shorter than its diff:
```python
import functools
import math

import jax
import jax.numpy as jnp
from jax import lax
from jax.experimental import pallas as pl
from jax.experimental.pallas import tpu as pltpu
from jax.sharding import PartitionSpec as P

MASK_FILL = -1e30
ROW_BLOCK = 64


def tick_kernel(tick, order_ref, q_ref, g_ref, kv_ref, *rest):
    dq_ref, terms_ref, s_ref, dp_ref, p_ref, ds_ref, acc_ref = rest[-7:]
    local_rows = q_ref.shape[2]
    key_rows = kv_ref.shape[0]
    head_dim = kv_ref.shape[1] // 2
    heads = q_ref.shape[3] // head_dim
    pairs = heads // 2
    width = 2 * local_rows
    scale = 1.0 / math.sqrt(head_dim)
    exp_scale = scale * math.log2(math.e)

    own_group = order_ref[lax.axis_index("ctx")]
    key_mat = kv_ref[:, :head_dim]
    value_mat = kv_ref[:, head_dim:]
    key_t = key_mat.T
    blocks_per_shard = local_rows // ROW_BLOCK
    row_iota = lax.broadcasted_iota(jnp.int32, (ROW_BLOCK, width), 0)
    col_iota = lax.broadcasted_iota(jnp.int32, (ROW_BLOCK, width), 1)
    row_minus_col = row_iota - lax.rem(col_iota, local_rows)

    def stacked(ref, pair):
        lo = 2 * pair * head_dim
        return jnp.concatenate(
            [ref[0, 0, :, lo : lo + head_dim], ref[0, 0, :, lo + head_dim : lo + 2 * head_dim]],
            axis=0,
        )

    blocks = range(key_rows // ROW_BLOCK)
    contract_last = (((1,), (1,)), ((), ()))
    for pair in range(pairs):
        q_pair = stacked(q_ref, pair)
        g_pair = stacked(g_ref, pair)
        s_ref[pair] = lax.dot_general(
            key_mat, q_pair, contract_last, preferred_element_type=jnp.float32
        )
        dp_ref[pair] = lax.dot_general(
            value_mat, g_pair, contract_last, preferred_element_type=jnp.float32
        )
        biggest = jnp.full((8, width), MASK_FILL, jnp.float32)
        for block in blocks:
            rows = slice(block * ROW_BLOCK, (block + 1) * ROW_BLOCK)
            shard, part = divmod(block, blocks_per_shard)
            limit = (own_group - order_ref[shard]) * local_rows - part * ROW_BLOCK
            scores = jnp.where(row_minus_col <= limit, s_ref[pair, rows], MASK_FILL)
            s_ref[pair, rows] = scores
            biggest = jnp.maximum(
                biggest, jnp.max(scores.reshape(ROW_BLOCK // 8, 8, width), axis=0)
            )
        shift = jnp.max(biggest, axis=0, keepdims=True) * exp_scale
        total = jnp.zeros((8, width), jnp.float32)
        weighted = jnp.zeros((8, width), jnp.float32)
        for block in blocks:
            rows = slice(block * ROW_BLOCK, (block + 1) * ROW_BLOCK)
            expo = jnp.exp2(s_ref[pair, rows] * exp_scale - shift)
            s_ref[pair, rows] = expo
            total = total + jnp.sum(expo.reshape(ROW_BLOCK // 8, 8, width), axis=0)
            weighted = weighted + jnp.sum(
                (expo * dp_ref[pair, rows]).reshape(ROW_BLOCK // 8, 8, width), axis=0
            )
        inverse = 1.0 / jnp.sum(total, axis=0, keepdims=True)
        delta = jnp.sum(weighted, axis=0, keepdims=True) * inverse
        for block in blocks:
            rows = slice(block * ROW_BLOCK, (block + 1) * ROW_BLOCK)
            probs = s_ref[pair, rows] * inverse
            p_ref[pair, rows] = probs.astype(jnp.bfloat16)
            ds_ref[pair, rows] = (probs * (dp_ref[pair, rows] - delta)).astype(jnp.bfloat16)
        score_grad = ds_ref[pair]
        key_terms = jnp.dot(score_grad, q_pair, preferred_element_type=jnp.float32)
        value_terms = jnp.dot(p_ref[pair], g_pair, preferred_element_type=jnp.float32)
        if pair == 0:
            acc_ref[:, :head_dim] = key_terms
            acc_ref[:, head_dim:] = value_terms
        elif pair < pairs - 1:
            acc_ref[:, :head_dim] += key_terms
            acc_ref[:, head_dim:] += value_terms
        else:
            terms_ref[:, :head_dim] = ((acc_ref[:, :head_dim] + key_terms) * scale).astype(
                terms_ref.dtype
            )
            terms_ref[:, head_dim:] = (acc_ref[:, head_dim:] + value_terms).astype(terms_ref.dtype)
        query_t = jnp.dot(key_t, score_grad, preferred_element_type=jnp.float32) * scale
        for half in range(2):
            lo = (2 * pair + half) * head_dim
            dq_ref[0, 0, :, lo : lo + head_dim] = query_t[
                :, half * local_rows : (half + 1) * local_rows
            ].T.astype(dq_ref.dtype)


def attend_back(tick, group_order, queries, out_grad, kv, query_grads):
    ticks, _, local_rows, model = queries.shape
    key_rows, width = kv.shape[0], kv.shape[1] // ticks
    head_dim = width // 2
    pairs = model // head_dim // 2
    tick_block = pl.BlockSpec((1, 1, local_rows, model), lambda i: (tick, 0, 0, 0))
    operands = [group_order, queries, out_grad, kv]
    in_specs = [
        pl.BlockSpec(memory_space=pltpu.SMEM),
        tick_block,
        tick_block,
        pl.BlockSpec((key_rows, width), lambda i: (0, tick)),
    ]
    aliases = {}
    if query_grads is not None:
        operands.append(query_grads)
        in_specs.append(pl.BlockSpec(memory_space=pl.ANY))
        aliases = {4: 0}
    tile = (pairs, key_rows, 2 * local_rows)
    return pl.pallas_call(
        functools.partial(tick_kernel, tick),
        grid=(1,),
        out_shape=(
            jax.ShapeDtypeStruct(queries.shape, jnp.bfloat16),
            jax.ShapeDtypeStruct((key_rows, width), jnp.bfloat16),
        ),
        in_specs=in_specs,
        out_specs=(tick_block, pl.BlockSpec((key_rows, width), lambda i: (0, 0))),
        scratch_shapes=[
            pltpu.VMEM(tile, jnp.float32),
            pltpu.VMEM(tile, jnp.float32),
            pltpu.VMEM(tile, jnp.bfloat16),
            pltpu.VMEM(tile, jnp.bfloat16),
            pltpu.VMEM((key_rows, width), jnp.float32),
        ],
        input_output_aliases=aliases,
        compiler_params=pltpu.CompilerParams(vmem_limit_bytes=44 * 2**20),
        cost_estimate=pl.CostEstimate(
            flops=10 * model * key_rows * local_rows,
            bytes_accessed=6 * local_rows * model + 4 * key_rows * width,
            transcendentals=model // head_dim * key_rows * local_rows,
        ),
    )(*operands)


def body(
    queries,
    out_grad,
    keys,
    values,
    entering_keys,
    entering_values,
    key_grads_in,
    value_grads_in,
    group_order,
):
    local_rows, head_dim = keys.shape[1:]
    ctx_count = lax.axis_size("ctx")
    sections = lax.axis_size("section")
    section = lax.axis_index("section")

    own_pair = jnp.concatenate([keys[0], values[0]], axis=1)
    entering_pair = jnp.concatenate([entering_keys, entering_values], axis=1)
    leaving_pair = jnp.where(section == 0, entering_pair, own_pair)
    next_pair = lax.ppermute(
        leaving_pair, "section", [(i, (i - 1) % sections) for i in range(sections)]
    )
    gathered = lax.all_gather(
        jnp.concatenate([own_pair, next_pair], axis=1), "ctx", axis=0, tiled=True
    )

    def reduced(terms):
        pieces = lax.all_to_all(
            terms.reshape(ctx_count, local_rows, 2 * head_dim),
            "ctx",
            split_axis=0,
            concat_axis=0,
            tiled=True,
        )
        return jnp.sum(pieces.astype(jnp.float32), axis=0)

    query_grads, terms = attend_back(0, group_order, queries, out_grad, gathered, None)
    first_acc = jnp.concatenate([key_grads_in[0], value_grads_in[0]], axis=1) + reduced(terms)
    moved_acc = lax.ppermute(first_acc, "section", [(i, i - 1) for i in range(1, sections)])
    query_grads, terms = attend_back(1, group_order, queries, out_grad, gathered, query_grads)
    second_acc = moved_acc + reduced(terms)
    key_grads = jnp.stack([first_acc[:, :head_dim], second_acc[:, :head_dim]], axis=0)[:, None]
    value_grads = jnp.stack([first_acc[:, head_dim:], second_acc[:, head_dim:]], axis=0)[:, None]
    return (query_grads, key_grads, value_grads)


def solution(mesh):
    return jax.shard_map(
        body,
        mesh=mesh,
        in_specs=(
            P(None, "section", "ctx", None),
            P(None, "section", "ctx", None),
            P("section", "ctx", None),
            P("section", "ctx", None),
            P("ctx", None),
            P("ctx", None),
            P("section", "ctx", None),
            P("section", "ctx", None),
            P(),
        ),
        out_specs=(
            P(None, "section", "ctx", None),
            P(None, "section", "ctx", None),
            P(None, "section", "ctx", None),
        ),
        check_vma=False,
    )
```

time: 126 us -> 93.8 us (0.74)
  blocking collectives: 33.3 us -> 0 us
  matrix products: 16.9 us -> 0 us
  waiting for transfers between devices: 31.9 us -> 48.7 us
  Pallas kernels: 0 us -> 11.8 us
  other arithmetic: 14.6 us -> 3.22 us
  starting transfers between devices: 2.66 us -> 12.4 us
  local copies, waits for them, and re-layouts: 9.7 us -> 3.09 us
  between operations: 15.5 us -> 14.1 us
    all_gather x2 -> x0, blocking collectives: 33.3 us -> none  [one_tick(): grad_kv_piece = lax.all_gather(kv_pair, 'ctx', axis=0, tiled=True)]
    reduce_scatter x2 -> x0, waiting for transfers between devices: 28.2 us -> none  [one_tick(): summed = lax.psum_scatter(terms, 'ctx', scatter_dimension=0, tiled=True)]
    all_gather x0 -> x1, waiting for transfers between devices: none -> 24.3 us  [body(): lax.all_gather(jnp.concatenate([own_pair, next_pair], axis=1), 'ctx', axi...]
    all_to_all x0 -> x2, waiting for transfers between devices: none -> 22.4 us  [reduced(): lax.all_to_all(terms.reshape(ctx_count, local_rows, 2 * head_dim), 'ctx',...]
    dot_general x14 -> x0, matrix products: 16.9 us -> none  [the longest x4 6.07 us: masked_scores(): jnp.dot(queries_flat, kv_piece[:, :head_dim].T, preferred_element_type=jn...]
    pallas_call x0 -> x2, Pallas kernels: none -> 11.8 us  [attend_back(): pl.pallas_call(functools.partial(tick_kernel, tick), grid=(1,), out_shape...]
    all_to_all x0 -> x2, starting transfers between devices: none -> 7.12 us  [reduced(): lax.all_to_all(terms.reshape(ctx_count, local_rows, 2 * head_dim), 'ctx',...]
    reduce_sum x4 -> x2, other arithmetic: 5.87 us -> 0.14 us  [reduced(): return jnp.sum(pieces.astype(jnp.float32), axis=0)]
  transfers between devices with their start and end apart: 4 -> 5, of which waited for: 2 -> 4; matrix products, arithmetic and copies ran while one was open for 15% -> 0% of each run, Pallas kernels for 0% -> 6%
where the time goes in v1:
time: 93.8 us; the launch traced here: 93.3 us
  waiting for transfers between devices  48.7 us (52%)
  between operations  14.1 us (15%)
  starting transfers between devices  12.4 us (13%)
  Pallas kernels  11.8 us (13%)
  other arithmetic  3.22 us (3%)
  local copies, waits for them, and re-layouts  3.09 us (3%)
    all_gather x1, waiting for transfers between devices, body(): lax.all_gather(jnp.concatenate([own_pair, next_pair], axis=1), 'ctx', axi...  24.3 us
    all_to_all x2, waiting for transfers between devices, reduced(): lax.all_to_all(terms.reshape(ctx_count, local_rows, 2 * head_dim), 'ctx',...  22.4 us
    pallas_call x2, Pallas kernels, attend_back(): pl.pallas_call(functools.partial(tick_kernel, tick), grid=(1,), out_shape...  11.8 us
    all_to_all x2, starting transfers between devices, reduced(): lax.all_to_all(terms.reshape(ctx_count, local_rows, 2 * head_dim), 'ctx',...  7.12 us
    ppermute x1, starting transfers between devices, body(): lax.ppermute(leaving_pair, 'section', [(i, (i - 1) % sections) for i in r...  3.95 us
    unnamed x16, local copies, waits for them, and re-layouts  3.06 us
    ppermute x1, waiting for transfers between devices, body(): lax.ppermute(leaving_pair, 'section', [(i, (i - 1) % sections) for i in r...  1.91 us
  transfers between devices with their start and end apart: 5, of which 4 were waited for; matrix products, arithmetic and copies ran while one was open for 0% of the time, Pallas kernels for 6%

profile of v1, /device:TPU:0, one launch (start us, length us, event | category | flops | bytes accessed | tf_op | source)
XLA Modules:
  0.0 93.3 jit_solution(5480070934341074880)
XLA Ops:
  7.2 0.0 all-gather.2.cloned.1.call-start
  7.2 0.9 maximum_select_fusion
  8.1 3.9 %collective-permute-start = (bf16[128,256]{1,0:T(8,128)(2,1)S(1)}, bf16[128,256]{1,0:T(8,128)(2,1)S(1)}, u32[]{:S(2)}, u32[]{:S(2)}) collective-permute-start(bf16[128,256]{1,0:T(8,128)(2,1)S(1)} %maximum_select_fusion), channel_id=1, source_target_pairs={{0,24},{8,0},{16,8},{24,16},{1,25},{9,1},{17,9},{25,17},{2,26},{10... | collective-permute-start | bytes 196616 | tf_op jit(solution)/shard_map/ppermute | solution.py:167
  12.1 1.9 %collective-permute-done = bf16[128,256]{1,0:T(8,128)(2,1)S(1)} collective-permute-done((bf16[128,256]{1,0:T(8,128)(2,1)S(1)}, bf16[128,256]{1,0:T(8,128)(2,1)S(1)}, u32[]{:S(2)}, u32[]{:S(2)}) %collective-permute-start) | collective-permute-done | bytes 65568 | tf_op jit(solution)/shard_map/ppermute | solution.py:167
  14.0 1.4 %pad_maximum_fusion = bf16[128,512]{1,0:T(8,128)(2,1)} fusion(bf16[128,256]{1,0:T(8,128)(2,1)S(1)} %collective-permute-done, bf16[128,128]{1,0:T(8,128)(2,1)} %bitcast.19, bf16[128,128]{1,0:T(8,128)(2,1)} %bitcast.21), kind=kLoop, calls=%fused_computation.2 | loop fusion | flops 393216 | bytes 262144 | tf_op jit(solution)/shard_map/concatenate | solution.py:171
  15.4 0.0 all-gather.2.cloned.1.call-update
  15.4 24.3 %all-gather.2.cloned.1.call-done.kv_ref = bf16[1024,512]{1,0:T(8,128)(2,1)} async-done(((bf16[128,512]{1,0:T(8,128)(2,1)}), bf16[1024,512]{1,0:T(8,128)(2,1)}) %all-gather.2.cloned.1.call-update) | async-done | bytes 1048592 | tf_op jit(solution)/shard_map/all_gather | solution.py:170
  39.8 1.2 %copy-done = bf16[1024,512]{1,0:T(8,128)(2,1)S(1)} copy-done((bf16[1024,512]{1,0:T(8,128)(2,1)S(1)}, bf16[1024,512]{1,0:T(8,128)(2,1)}, u32[]{:S(2)}) %copy-start) | copy-done | bytes 1048600
  41.0 1.0 %copy-done.3 = bf16[2,1,128,1024]{3,2,1,0:T(8,128)(2,1)S(1)} copy-done((bf16[2,1,128,1024]{3,2,1,0:T(8,128)(2,1)S(1)}, bf16[2,1,128,1024]{3,2,1,0:T(8,128)(2,1)}, u32[]{:S(2)}) %copy-start.3) | copy-done | bytes 524312
  42.0 5.9 %shard_map.112 = (bf16[2,1,128,1024]{3,2,1,0:T(8,128)(2,1)}, bf16[1024,256]{1,0:T(8,128)(2,1)}) custom-call(s32[8]{0:T(128)S(1)} %copy-done.5, bf16[2,1,128,1024]{3,2,1,0:T(8,128)(2,1)S(1)} %copy-done.2, bf16[2,1,128,1024]{3,2,1,0:T(8,128)(2,1)S(1)} %copy-done.3, bf16[1024,512]{1,0:T(8,128)(2,1)S(1)} %copy-done), custom_call_target="tpu_custom_call" | custom-call | flops 1342177280 | bytes 1835008 | tf_op jit(solution)/shard_map/pallas_call | solution.py:122
  47.9 3.6 %all-to-all-start = ((bf16[8,128,256]{2,1,0:T(8,128)(2,1)}), bf16[8,128,256]{2,1,0:T(8,128)(2,1)S(1)}, u32[]{:S(2)}, u32[]{:S(2)}) async-start(bf16[8,128,256]{2,1,0:T(8,128)(2,1)} %bitcast.4), calls=%async_computation | async-start | bytes 1048576 | tf_op jit(solution)/shard_map/all_to_all | solution.py:175
  51.6 5.9 %shard_map.113 = (bf16[2,1,128,1024]{3,2,1,0:T(8,128)(2,1)}, bf16[1024,256]{1,0:T(8,128)(2,1)}) custom-call(s32[8]{0:T(128)S(1)} %copy-done.5, bf16[2,1,128,1024]{3,2,1,0:T(8,128)(2,1)S(1)} %copy-done.2, bf16[2,1,128,1024]{3,2,1,0:T(8,128)(2,1)S(1)} %copy-done.4, bf16[1024,512]{1,0:T(8,128)(2,1)S(1)} %copy-done.1, ...), custom_call_target="tpu_custom_call", output_to_operand_aliasing={{0}: (4, {})} | custom-call | flops 1342177280 | bytes 1835008 | tf_op jit(solution)/shard_map/pallas_call | solution.py:122
  57.4 9.4 %all-to-all-done = bf16[8,128,256]{2,1,0:T(8,128)(2,1)S(1)} async-done(((bf16[8,128,256]{2,1,0:T(8,128)(2,1)}), bf16[8,128,256]{2,1,0:T(8,128)(2,1)S(1)}, u32[]{:S(2)}, u32[]{:S(2)}) %all-to-all-start) | async-done | bytes 524320 | tf_op jit(solution)/shard_map/all_to_all | solution.py:175
  66.8 3.5 %all-to-all-start.1 = ((bf16[8,128,256]{2,1,0:T(8,128)(2,1)}), bf16[8,128,256]{2,1,0:T(8,128)(2,1)S(1)}, u32[]{:S(2)}, u32[]{:S(2)}) async-start(bf16[8,128,256]{2,1,0:T(8,128)(2,1)} %bitcast.6), calls=%async_computation.1 | async-start | bytes 1048576 | tf_op jit(solution)/shard_map/all_to_all | solution.py:175
  70.3 0.0 copy-start.6
  70.3 0.0 copy-start.7
  70.3 0.1 convert_reduce_fusion.1
  70.4 0.7 copy-done.6
  71.2 0.0 copy-done.7
  71.2 1.3 %collective-permute-start.1 = (f32[128,256]{1,0:T(8,128)S(1)}, f32[128,256]{1,0:T(8,128)S(1)}, u32[]{:S(2)}, u32[]{:S(2)}) collective-permute-start(f32[128,256]{1,0:T(8,128)S(1)} %maximum_add_fusion), channel_id=1, source_target_pairs={{8,0},{16,8},{24,16},{9,1},{17,9},{25,17},{10,2},{18,10},{26,18},{... | collective-permute-start | bytes 393224 | tf_op jit(solution)/shard_map/ppermute | solution.py:186
  72.5 13.1 %all-to-all-done.1 = bf16[8,128,256]{2,1,0:T(8,128)(2,1)S(1)} async-done(((bf16[8,128,256]{2,1,0:T(8,128)(2,1)}), bf16[8,128,256]{2,1,0:T(8,128)(2,1)S(1)}, u32[]{:S(2)}, u32[]{:S(2)}) %all-to-all-start.1) | async-done | bytes 524320 | tf_op jit(solution)/shard_map/all_to_all | solution.py:175
  85.6 0.1 convert_reduce_fusion
  85.7 0.0 collective-permute-done.1
  85.7 0.7 maximum_bitcast_fusion
  (14 shorter events, 0.1 us)
Async XLA Ops:
  7.2 32.6 %copy-start.2 = (bf16[2,1,128,1024]{3,2,1,0:T(8,128)(2,1)S(1)}, bf16[2,1,128,1024]{3,2,1,0:T(8,128)(2,1)}, u32[]{:S(2)}) copy-start(bf16[2,1,128,1024]{3,2,1,0:T(8,128)(2,1)} %q_ref.3) | copy-start | bytes 1572868
  7.2 32.6 %all-gather.2.cloned.1.call-start = ((), (), s32[]{:S(2)}) async-start(), calls=%async_computation.2 | async-start | bytes 1179648 | tf_op jit(solution)/shard_map/all_gather | solution.py:170
  8.1 5.9 %collective-permute-start = (bf16[128,256]{1,0:T(8,128)(2,1)S(1)}, bf16[128,256]{1,0:T(8,128)(2,1)S(1)}, u32[]{:S(2)}, u32[]{:S(2)}) collective-permute-start(bf16[128,256]{1,0:T(8,128)(2,1)S(1)} %maximum_select_fusion), channel_id=1, source_target_pairs={{0,24},{8,0},{16,8},{24,16},{1,25},{9,1},{17,9},{25,17},{2,26},{10... | collective-permute-start | bytes 196616 | tf_op jit(solution)/shard_map/ppermute | solution.py:167
  15.4 24.4 %copy-start.5 = (s32[8]{0:T(128)S(1)}, s32[8]{0:T(128)}, u32[]{:S(2)}) copy-start(s32[8]{0:T(128)} %order_ref.3) | copy-start | bytes 100
  39.7 1.2 %copy-start = (bf16[1024,512]{1,0:T(8,128)(2,1)S(1)}, bf16[1024,512]{1,0:T(8,128)(2,1)}, u32[]{:S(2)}) copy-start(bf16[1024,512]{1,0:T(8,128)(2,1)} %all-gather.2.cloned.1.call-done.kv_ref) | copy-start | bytes 3145732
  41.0 1.0 %copy-start.3 = (bf16[2,1,128,1024]{3,2,1,0:T(8,128)(2,1)S(1)}, bf16[2,1,128,1024]{3,2,1,0:T(8,128)(2,1)}, u32[]{:S(2)}) copy-start(bf16[2,1,128,1024]{3,2,1,0:T(8,128)(2,1)} %g_ref.3) | copy-start | bytes 1572868
  42.0 9.5 %copy-start.4 = (bf16[2,1,128,1024]{3,2,1,0:T(8,128)(2,1)S(1)}, bf16[2,1,128,1024]{3,2,1,0:T(8,128)(2,1)}, u32[]{:S(2)}) copy-start(bf16[2,1,128,1024]{3,2,1,0:T(8,128)(2,1)} %g_ref.3) | copy-start | bytes 1572868
  47.9 3.6 %copy-start.1 = (bf16[1024,512]{1,0:T(8,128)(2,1)S(1)}, bf16[1024,512]{1,0:T(8,128)(2,1)}, u32[]{:S(2)}) copy-start(bf16[1024,512]{1,0:T(8,128)(2,1)} %all-gather.2.cloned.1.call-done.kv_ref) | copy-start | bytes 3145732
  47.9 18.9 %all-to-all-start = ((bf16[8,128,256]{2,1,0:T(8,128)(2,1)}), bf16[8,128,256]{2,1,0:T(8,128)(2,1)S(1)}, u32[]{:S(2)}, u32[]{:S(2)}) async-start(bf16[8,128,256]{2,1,0:T(8,128)(2,1)} %bitcast.4), calls=%async_computation | async-start | bytes 1048576 | tf_op jit(solution)/shard_map/all_to_all | solution.py:175
  66.8 18.8 %all-to-all-start.1 = ((bf16[8,128,256]{2,1,0:T(8,128)(2,1)}), bf16[8,128,256]{2,1,0:T(8,128)(2,1)S(1)}, u32[]{:S(2)}, u32[]{:S(2)}) async-start(bf16[8,128,256]{2,1,0:T(8,128)(2,1)} %bitcast.6), calls=%async_computation.1 | async-start | bytes 1048576 | tf_op jit(solution)/shard_map/all_to_all | solution.py:175
  70.3 0.8 copy-start.6
  70.3 0.9 copy-start.7
  71.2 14.5 %collective-permute-start.1 = (f32[128,256]{1,0:T(8,128)S(1)}, f32[128,256]{1,0:T(8,128)S(1)}, u32[]{:S(2)}, u32[]{:S(2)}) collective-permute-start(f32[128,256]{1,0:T(8,128)S(1)} %maximum_add_fusion), channel_id=1, source_target_pairs={{8,0},{16,8},{24,16},{9,1},{17,9},{25,17},{10,2},{18,10},{26,18},{... | collective-permute-start | bytes 393224 | tf_op jit(solution)/shard_map/ppermute | solution.py:186
Sparse Core Ops, SparseCore 0:
  15.5 24.1 all-gather.1

commit v2 on v1

--- a/solution.py
+++ b/solution.py
@@ -1,4 +1,3 @@
-import functools
 import math
 
 import jax
@@ -12,22 +11,31 @@
 ROW_BLOCK = 64
 
 
-def tick_kernel(tick, order_ref, q_ref, g_ref, kv_ref, *rest):
-    dq_ref, terms_ref, s_ref, dp_ref, p_ref, ds_ref, acc_ref = rest[-7:]
+def tick_kernel(order_ref, q_ref, g_ref, near_ref, far_ref, *rest):
+    dq_ref, near_out_ref, far_out_ref, s_ref, dp_ref, p_ref, ds_ref, acc_ref = rest[-8:]
     local_rows = q_ref.shape[2]
-    key_rows = kv_ref.shape[0]
-    head_dim = kv_ref.shape[1] // 2
+    half_rows = near_ref.shape[0]
+    key_rows = 2 * half_rows
+    head_dim = near_ref.shape[1] // 2
     heads = q_ref.shape[3] // head_dim
     pairs = heads // 2
     width = 2 * local_rows
     scale = 1.0 / math.sqrt(head_dim)
     exp_scale = scale * math.log2(math.e)
 
-    own_group = order_ref[lax.axis_index("ctx")]
-    key_mat = kv_ref[:, :head_dim]
-    value_mat = kv_ref[:, head_dim:]
+    core = lax.axis_index("core")
+    own_group = order_ref[2 * lax.axis_index("z") + core]
+    key_mat = jnp.concatenate([near_ref[:, :head_dim], far_ref[:, :head_dim]], axis=0)
+    value_mat = jnp.concatenate([near_ref[:, head_dim:], far_ref[:, head_dim:]], axis=0)
     key_t = key_mat.T
     blocks_per_shard = local_rows // ROW_BLOCK
+    chips = half_rows // local_rows
+
+    def shard_id(slot):
+        if slot < chips:
+            return 2 * slot + core
+        return 2 * (slot - chips) + 1 - core
+
     row_iota = lax.broadcasted_iota(jnp.int32, (ROW_BLOCK, width), 0)
     col_iota = lax.broadcasted_iota(jnp.int32, (ROW_BLOCK, width), 1)
     row_minus_col = row_iota - lax.rem(col_iota, local_rows)
@@ -54,7 +62,7 @@
         for block in blocks:
             rows = slice(block * ROW_BLOCK, (block + 1) * ROW_BLOCK)
             shard, part = divmod(block, blocks_per_shard)
-            limit = (own_group - order_ref[shard]) * local_rows - part * ROW_BLOCK
+            limit = (own_group - order_ref[shard_id(shard)]) * local_rows - part * ROW_BLOCK
             scores = jnp.where(row_minus_col <= limit, s_ref[pair, rows], MASK_FILL)
             s_ref[pair, rows] = scores
             biggest = jnp.maximum(
@@ -88,10 +96,12 @@
             acc_ref[:, :head_dim] += key_terms
             acc_ref[:, head_dim:] += value_terms
         else:
-            terms_ref[:, :head_dim] = ((acc_ref[:, :head_dim] + key_terms) * scale).astype(
-                terms_ref.dtype
-            )
-            terms_ref[:, head_dim:] = (acc_ref[:, head_dim:] + value_terms).astype(terms_ref.dtype)
+            key_terms = (acc_ref[:, :head_dim] + key_terms) * scale
+            value_terms = acc_ref[:, head_dim:] + value_terms
+            near_out_ref[:, :head_dim] = key_terms[:half_rows].astype(near_out_ref.dtype)
+            near_out_ref[:, head_dim:] = value_terms[:half_rows].astype(near_out_ref.dtype)
+            far_out_ref[:, :head_dim] = key_terms[half_rows:].astype(far_out_ref.dtype)
+            far_out_ref[:, head_dim:] = value_terms[half_rows:].astype(far_out_ref.dtype)
         query_t = jnp.dot(key_t, score_grad, preferred_element_type=jnp.float32) * scale
         for half in range(2):
             lo = (2 * pair + half) * head_dim
@@ -100,34 +110,38 @@
             ].T.astype(dq_ref.dtype)
 
 
-def attend_back(tick, group_order, queries, out_grad, kv, query_grads):
-    ticks, _, local_rows, model = queries.shape
-    key_rows, width = kv.shape[0], kv.shape[1] // ticks
+def attend_back(tick, group_order, queries, out_grad, near, far, query_grads):
+    local_rows, model = queries.shape[2:]
+    half_rows, width = near.shape
+    key_rows = 2 * half_rows
     head_dim = width // 2
     pairs = model // head_dim // 2
     tick_block = pl.BlockSpec((1, 1, local_rows, model), lambda i: (tick, 0, 0, 0))
-    operands = [group_order, queries, out_grad, kv]
+    half_block = pl.BlockSpec((half_rows, width), lambda i: (0, 0))
+    operands = [group_order, queries, out_grad, near, far]
     in_specs = [
         pl.BlockSpec(memory_space=pltpu.SMEM),
         tick_block,
         tick_block,
-        pl.BlockSpec((key_rows, width), lambda i: (0, tick)),
+        half_block,
+        half_block,
     ]
     aliases = {}
     if query_grads is not None:
+        aliases = {len(operands): 0}
         operands.append(query_grads)
         in_specs.append(pl.BlockSpec(memory_space=pl.ANY))
-        aliases = {4: 0}
     tile = (pairs, key_rows, 2 * local_rows)
     return pl.pallas_call(
-        functools.partial(tick_kernel, tick),
+        tick_kernel,
         grid=(1,),
         out_shape=(
             jax.ShapeDtypeStruct(queries.shape, jnp.bfloat16),
-            jax.ShapeDtypeStruct((key_rows, width), jnp.bfloat16),
+            jax.ShapeDtypeStruct((half_rows, width), jnp.float32),
+            jax.ShapeDtypeStruct((half_rows, width), jnp.bfloat16),
         ),
         in_specs=in_specs,
-        out_specs=(tick_block, pl.BlockSpec((key_rows, width), lambda i: (0, 0))),
+        out_specs=(tick_block, half_block, half_block),
         scratch_shapes=[
             pltpu.VMEM(tile, jnp.float32),
             pltpu.VMEM(tile, jnp.float32),
@@ -139,10 +153,18 @@
         compiler_params=pltpu.CompilerParams(vmem_limit_bytes=44 * 2**20),
         cost_estimate=pl.CostEstimate(
             flops=10 * model * key_rows * local_rows,
-            bytes_accessed=6 * local_rows * model + 4 * key_rows * width,
+            bytes_accessed=6 * local_rows * model + 5 * key_rows * width,
             transcendentals=model // head_dim * key_rows * local_rows,
         ),
     )(*operands)
+
+
+def other_core(block):
+    return lax.ppermute(block, "core", [(0, 1), (1, 0)])
+
+
+def along_chips(blocks):
+    return lax.all_to_all(blocks, "z", split_axis=0, concat_axis=0, tiled=True)
 
 
 def body(
@@ -157,7 +179,8 @@
     group_order,
 ):
     local_rows, head_dim = keys.shape[1:]
-    ctx_count = lax.axis_size("ctx")
+    width = 2 * head_dim
+    chips = lax.axis_size("z")
     sections = lax.axis_size("section")
     section = lax.axis_index("section")
 
@@ -167,49 +190,57 @@
     next_pair = lax.ppermute(
         leaving_pair, "section", [(i, (i - 1) % sections) for i in range(sections)]
     )
-    gathered = lax.all_gather(
-        jnp.concatenate([own_pair, next_pair], axis=1), "ctx", axis=0, tiled=True
-    )
-
-    def reduced(terms):
-        pieces = lax.all_to_all(
-            terms.reshape(ctx_count, local_rows, 2 * head_dim),
-            "ctx",
-            split_axis=0,
-            concat_axis=0,
-            tiled=True,
+
+    def gathered(pair):
+        near = along_chips(jnp.broadcast_to(pair, (chips, local_rows, width)))
+        near = near.reshape(chips * local_rows, width)
+        return near, other_core(near)
+
+    def reduced(near_terms, far_terms):
+        chip_terms = near_terms + other_core(far_terms).astype(jnp.float32)
+        pieces = along_chips(
+            chip_terms.astype(jnp.bfloat16).reshape(chips, local_rows, width)
         )
         return jnp.sum(pieces.astype(jnp.float32), axis=0)
 
-    query_grads, terms = attend_back(0, group_order, queries, out_grad, gathered, None)
-    first_acc = jnp.concatenate([key_grads_in[0], value_grads_in[0]], axis=1) + reduced(terms)
+    first_kv = gathered(own_pair)
+    second_kv = gathered(next_pair)
+    query_grads, near, far = attend_back(0, group_order, queries, out_grad, *first_kv, None)
+    first_acc = jnp.concatenate([key_grads_in[0], value_grads_in[0]], axis=1) + reduced(near, far)
     moved_acc = lax.ppermute(first_acc, "section", [(i, i - 1) for i in range(1, sections)])
-    query_grads, terms = attend_back(1, group_order, queries, out_grad, gathered, query_grads)
-    second_acc = moved_acc + reduced(terms)
+    query_grads, near, far = attend_back(
+        1, group_order, queries, out_grad, *second_kv, query_grads
+    )
+    second_acc = moved_acc + reduced(near, far)
     key_grads = jnp.stack([first_acc[:, :head_dim], second_acc[:, :head_dim]], axis=0)[:, None]
     value_grads = jnp.stack([first_acc[:, head_dim:], second_acc[:, head_dim:]], axis=0)[:, None]
     return (query_grads, key_grads, value_grads)
 
 
 def solution(mesh):
+    sections, ctx_count = mesh.shape["section"], mesh.shape["ctx"]
+    chip_mesh = jax.sharding.Mesh(
+        mesh.devices.reshape(sections, ctx_count // 2, 2), ("section", "z", "core")
+    )
+    tokens = ("z", "core")
     return jax.shard_map(
         body,
-        mesh=mesh,
+        mesh=chip_mesh,
         in_specs=(
-            P(None, "section", "ctx", None),
-            P(None, "section", "ctx", None),
-            P("section", "ctx", None),
-            P("section", "ctx", None),
-            P("ctx", None),
-            P("ctx", None),
-            P("section", "ctx", None),
-            P("section", "ctx", None),
+            P(None, "section", tokens, None),
+            P(None, "section", tokens, None),
+            P("section", tokens, None),
+            P("section", tokens, None),
+            P(tokens, None),
+            P(tokens, None),
+            P("section", tokens, None),
+            P("section", tokens, None),
             P(),
         ),
         out_specs=(
-            P(None, "section", "ctx", None),
-            P(None, "section", "ctx", None),
-            P(None, "section", "ctx", None),
+            P(None, "section", tokens, None),
+            P(None, "section", tokens, None),
+            P(None, "section", tokens, None),
         ),
         check_vma=False,
     )

time: 93.8 us -> 67.8 us (0.72)
  waiting for transfers between devices: 48.7 us -> 28.3 us
  between operations: 14.1 us -> 0.78 us
  starting transfers between devices: 12.4 us -> 21 us
    all_gather x1 -> x0, waiting for transfers between devices: 24.3 us -> none  [body(): lax.all_gather(jnp.concatenate([own_pair, next_pair], axis=1), 'ctx', axi...]
    all_to_all x2 -> x4, starting transfers between devices: 7.12 us -> 16.7 us  [along_chips(): return lax.all_to_all(blocks, 'z', split_axis=0, concat_axis=0, tiled=True)]
    all_to_all x2 -> x4, waiting for transfers between devices: 22.4 us -> 26.4 us  [along_chips(): return lax.all_to_all(blocks, 'z', split_axis=0, concat_axis=0, tiled=True)]
    unnamed x16 -> x10, local copies, waits for them, and re-layouts: 3.06 us -> 0.83 us
    ppermute x1, starting transfers between devices: 3.95 us -> 2.45 us  [body(): lax.ppermute(leaving_pair, 'section', [(i, (i - 1) % sections) for i in r...]
    convert_element_type x0 -> x2, other arithmetic: none -> 1.49 us  [reduced(): chip_terms.astype(jnp.bfloat16).reshape(chips, local_rows, width)]
    broadcast_in_dim x0 -> x2, local copies, waits for them, and re-layouts: none -> 1.44 us  [gathered(): near = along_chips(jnp.broadcast_to(pair, (chips, local_rows, width)))]
  transfers between devices with their start and end apart: 5 -> 10, of which waited for: 4 -> 5; matrix products, arithmetic and copies ran while one was open for 0% -> 2% of each run, Pallas kernels for 6% -> 17%
where the time goes in v2:
time: 67.8 us; the launch traced here: 67.2 us
  waiting for transfers between devices  28.3 us (42%)
  starting transfers between devices  21 us (31%)
  Pallas kernels  11.7 us (17%)
  other arithmetic  3.17 us (5%)
  local copies, waits for them, and re-layouts  2.29 us (3%)
  between operations  0.78 us (1%)
    all_to_all x4, waiting for transfers between devices, along_chips(): return lax.all_to_all(blocks, 'z', split_axis=0, concat_axis=0, tiled=True)  26.4 us
    all_to_all x4, starting transfers between devices, along_chips(): return lax.all_to_all(blocks, 'z', split_axis=0, concat_axis=0, tiled=True)  16.7 us
    pallas_call x2, Pallas kernels, attend_back(): pl.pallas_call(tick_kernel, grid=(1,), out_shape=(jax.ShapeDtypeStruct(qu...  11.7 us
    ppermute x1, starting transfers between devices, body(): lax.ppermute(leaving_pair, 'section', [(i, (i - 1) % sections) for i in r...  2.45 us
    ppermute x1, waiting for transfers between devices, body(): lax.ppermute(leaving_pair, 'section', [(i, (i - 1) % sections) for i in r...  1.91 us
    convert_element_type x2, other arithmetic, reduced(): chip_terms.astype(jnp.bfloat16).reshape(chips, local_rows, width)  1.49 us
    broadcast_in_dim x2, local copies, waits for them, and re-layouts, gathered(): near = along_chips(jnp.broadcast_to(pair, (chips, local_rows, width)))  1.44 us
  transfers between devices with their start and end apart: 10, of which 5 were waited for; matrix products, arithmetic and copies ran while one was open for 2% of the time, Pallas kernels for 17%

profile of v2, /device:TPU:0, one launch (start us, length us, event | category | flops | bytes accessed | tf_op | source)
XLA Modules:
  0.0 67.2 jit_solution(6684568130200015659)
XLA Ops:
  0.6 0.8 %pad_maximum_fusion = (bf16[128,256]{1,0:T(8,128)(2,1)S(1)}, bf16[128,256]{1,0:T(8,128)(2,1)S(1)}) fusion(bf16[128,128]{1,0:T(8,128)(2,1)} %bitcast.26, bf16[128,128]{1,0:T(8,128)(2,1)} %bitcast.27, bf16[128,128]{1,0:T(8,128)(2,1)} %param.14, bf16[128,128]{1,0:T(8,128)(2,1)} %param.13, pred[]{:T(512)S(6)} %eq.3), kind=kLoop, calls=%fused_computation.12 | loop fusion | flops 294912 | bytes 262145 | tf_op jit(solution)/shard_map/concatenate | solution.py:187
  1.5 0.7 %broadcast_in_dim.13 = bf16[4,128,256]{2,1,0:T(8,128)(2,1)} broadcast(bf16[128,256]{1,0:T(8,128)(2,1)S(1)} %get-tuple-element.19), dimensions={1,2} | broadcast | bytes 327680 | tf_op jit(solution)/shard_map/broadcast_in_dim | solution.py:195
  2.2 6.4 %all-to-all-start.1 = ((bf16[4,128,256]{2,1,0:T(8,128)(2,1)}), bf16[4,128,256]{2,1,0:T(8,128)(2,1)S(1)}, u32[]{:S(2)}, u32[]{:S(2)}) async-start(bf16[4,128,256]{2,1,0:T(8,128)(2,1)} %broadcast_in_dim.13), calls=%async_computation.1 | async-start | bytes 524288 | tf_op jit(solution)/shard_map/all_to_all | solution.py:167
  8.6 2.4 %collective-permute-start = (bf16[128,256]{1,0:T(8,128)(2,1)S(1)}, bf16[128,256]{1,0:T(8,128)(2,1)S(1)}, u32[]{:S(2)}, u32[]{:S(2)}) collective-permute-start(bf16[128,256]{1,0:T(8,128)(2,1)S(1)} %get-tuple-element.20), channel_id=1, source_target_pairs={{0,24},{8,0},{16,8},{24,16},{1,25},{9,1},{17,9},{25,17},{2,26},{10... | collective-permute-start | bytes 196616 | tf_op jit(solution)/shard_map/ppermute | solution.py:190
  11.1 1.9 %collective-permute-done = bf16[128,256]{1,0:T(8,128)(2,1)S(1)} collective-permute-done((bf16[128,256]{1,0:T(8,128)(2,1)S(1)}, bf16[128,256]{1,0:T(8,128)(2,1)S(1)}, u32[]{:S(2)}, u32[]{:S(2)}) %collective-permute-start) | collective-permute-done | bytes 65568 | tf_op jit(solution)/shard_map/ppermute | solution.py:190
  13.0 4.6 %all-to-all-done.1 = bf16[4,128,256]{2,1,0:T(8,128)(2,1)S(1)} async-done(((bf16[4,128,256]{2,1,0:T(8,128)(2,1)}), bf16[4,128,256]{2,1,0:T(8,128)(2,1)S(1)}, u32[]{:S(2)}, u32[]{:S(2)}) %all-to-all-start.1) | async-done | bytes 262176 | tf_op jit(solution)/shard_map/all_to_all | solution.py:167
  17.6 0.7 %broadcast_in_dim.12 = bf16[4,128,256]{2,1,0:T(8,128)(2,1)} broadcast(bf16[128,256]{1,0:T(8,128)(2,1)S(1)} %collective-permute-done), dimensions={1,2} | broadcast | bytes 327680 | tf_op jit(solution)/shard_map/broadcast_in_dim | solution.py:195
  18.3 3.4 %all-to-all-start = ((bf16[4,128,256]{2,1,0:T(8,128)(2,1)}), bf16[4,128,256]{2,1,0:T(8,128)(2,1)S(1)}, u32[]{:S(2)}, u32[]{:S(2)}) async-start(bf16[4,128,256]{2,1,0:T(8,128)(2,1)} %broadcast_in_dim.12), calls=%async_computation | async-start | bytes 524288 | tf_op jit(solution)/shard_map/all_to_all | solution.py:167
  21.7 0.1 collective-permute-start.2
  21.8 6.9 %all-to-all-done = bf16[4,128,256]{2,1,0:T(8,128)(2,1)S(1)} async-done(((bf16[4,128,256]{2,1,0:T(8,128)(2,1)}), bf16[4,128,256]{2,1,0:T(8,128)(2,1)S(1)}, u32[]{:S(2)}, u32[]{:S(2)}) %all-to-all-start) | async-done | bytes 262176 | tf_op jit(solution)/shard_map/all_to_all | solution.py:167
  28.7 5.8 %shard_map.112 = (bf16[2,1,128,1024]{3,2,1,0:T(8,128)(2,1)}, f32[512,256]{1,0:T(8,128)S(1)}, bf16[512,256]{1,0:T(8,128)(2,1)S(1)}) custom-call(s32[8]{0:T(128)S(1)} %copy-done.2, bf16[2,1,128,1024]{3,2,1,0:T(8,128)(2,1)S(1)} %copy-done, bf16[2,1,128,1024]{3,2,1,0:T(8,128)(2,1)S(1)} %copy-done.1, bf16[512,256]{1,0:T(8,128)(2,1)S(1)} %bitcast.21, ...), custom_call_target="tpu_custom_call" | custom-call | flops 1342177280 | bytes 2097152 | tf_op jit(solution)/shard_map/pallas_call | solution.py:135
  34.5 0.5 collective-permute-start.3
  35.0 5.8 %shard_map.113 = (bf16[2,1,128,1024]{3,2,1,0:T(8,128)(2,1)}, f32[512,256]{1,0:T(8,128)S(1)}, bf16[512,256]{1,0:T(8,128)(2,1)S(1)}) custom-call(s32[8]{0:T(128)S(1)} %copy-done.2, bf16[2,1,128,1024]{3,2,1,0:T(8,128)(2,1)S(1)} %copy-done, bf16[2,1,128,1024]{3,2,1,0:T(8,128)(2,1)S(1)} %copy-done.1, ...), custom_call_target="tpu_custom_call", output_to_operand_aliasing={{0}: (5, {})} | custom-call | flops 1342177280 | bytes 2097152 | tf_op jit(solution)/shard_map/pallas_call | solution.py:135
  40.9 0.0 collective-permute-start.5
  40.9 0.7 %add_convert_fusion.1 = bf16[512,256]{1,0:T(8,128)(2,1)} fusion(f32[512,256]{1,0:T(8,128)S(1)} %get-tuple-element.11, bf16[512,256]{1,0:T(8,128)(2,1)S(1)} %collective-permute-done.3), kind=kLoop, calls=%fused_computation.3 | loop fusion | flops 393216 | bytes 1048576 | tf_op jit(solution)/shard_map/convert_element_type | solution.py:202
  41.6 3.4 %all-to-all-start.2 = ((bf16[4,128,256]{2,1,0:T(8,128)(2,1)}), bf16[4,128,256]{2,1,0:T(8,128)(2,1)S(1)}, u32[]{:S(2)}, u32[]{:S(2)}) async-start(bf16[4,128,256]{2,1,0:T(8,128)(2,1)} %bitcast.6), calls=%async_computation.2 | async-start | bytes 524288 | tf_op jit(solution)/shard_map/all_to_all | solution.py:167
  45.1 0.7 %add_convert_fusion = bf16[512,256]{1,0:T(8,128)(2,1)} fusion(f32[512,256]{1,0:T(8,128)S(1)} %get-tuple-element.13, bf16[512,256]{1,0:T(8,128)(2,1)S(1)} %collective-permute-done.5), kind=kLoop, calls=%fused_computation.1 | loop fusion | flops 393216 | bytes 1048576 | tf_op jit(solution)/shard_map/convert_element_type | solution.py:202
  45.8 9.0 %all-to-all-done.2 = bf16[4,128,256]{2,1,0:T(8,128)(2,1)S(1)} async-done(((bf16[4,128,256]{2,1,0:T(8,128)(2,1)}), bf16[4,128,256]{2,1,0:T(8,128)(2,1)S(1)}, u32[]{:S(2)}, u32[]{:S(2)}) %all-to-all-start.2) | async-done | bytes 262176 | tf_op jit(solution)/shard_map/all_to_all | solution.py:167
  54.8 3.4 %all-to-all-start.3 = ((bf16[4,128,256]{2,1,0:T(8,128)(2,1)}), bf16[4,128,256]{2,1,0:T(8,128)(2,1)S(1)}, u32[]{:S(2)}, u32[]{:S(2)}) async-start(bf16[4,128,256]{2,1,0:T(8,128)(2,1)} %bitcast.8), calls=%async_computation.3 | async-start | bytes 524288 | tf_op jit(solution)/shard_map/all_to_all | solution.py:167
  58.3 0.8 %copy-done.3 = f32[1,128,128]{2,1,0:T(8,128)S(1)} copy-done((f32[1,128,128]{2,1,0:T(8,128)S(1)}, f32[1,128,128]{2,1,0:T(8,128)}, u32[]{:S(2)}) %copy-start.3) | copy-done | bytes 65560
  59.1 0.0 copy-done.4
  59.1 1.3 %collective-permute-start.4 = (f32[128,256]{1,0:T(8,128)S(1)}, f32[128,256]{1,0:T(8,128)S(1)}, u32[]{:S(2)}, u32[]{:S(2)}) collective-permute-start(f32[128,256]{1,0:T(8,128)S(1)} %maximum_add_fusion), channel_id=1, source_target_pairs={{8,0},{16,8},{24,16},{9,1},{17,9},{25,17},{10,2},{18,10},{26,18},{... | collective-permute-start | bytes 393224 | tf_op jit(solution)/shard_map/ppermute | solution.py:210
  60.5 5.9 %all-to-all-done.3 = bf16[4,128,256]{2,1,0:T(8,128)(2,1)S(1)} async-done(((bf16[4,128,256]{2,1,0:T(8,128)(2,1)}), bf16[4,128,256]{2,1,0:T(8,128)(2,1)S(1)}, u32[]{:S(2)}, u32[]{:S(2)}) %all-to-all-start.3) | async-done | bytes 262176 | tf_op jit(solution)/shard_map/all_to_all | solution.py:167
  66.5 0.7 %maximum_bitcast_fusion = (f32[2,1,128,128]{3,2,1,0:T(8,128)}, f32[2,1,128,128]{3,2,1,0:T(8,128)}) fusion(f32[1,128,128]{2,1,0:T(8,128)S(1)} %get-tuple-element.18, f32[1,128,128]{2,1,0:T(8,128)S(1)} %get-tuple-element.16, f32[1,128,128]{2,1,0:T(8,128)S(1)} %get-tuple-element.17, f32[1,128,128]{2,1,0:T(8,128)S(1)} %get-tuple-element.15), kind=kLoop, calls=%fused_computation.5 | loop fusion | flops 65536 | bytes 524288 | tf_op jit(solution)/shard_map/broadcast_in_dim | solution.py:215
  (20 shorter events, 0.2 us)
Async XLA Ops:
  2.2 26.5 %copy-start.1 = (bf16[2,1,128,1024]{3,2,1,0:T(8,128)(2,1)S(1)}, bf16[2,1,128,1024]{3,2,1,0:T(8,128)(2,1)}, u32[]{:S(2)}) copy-start(bf16[2,1,128,1024]{3,2,1,0:T(8,128)(2,1)} %g_ref.3) | copy-start | bytes 1572868
  2.2 15.4 %all-to-all-start.1 = ((bf16[4,128,256]{2,1,0:T(8,128)(2,1)}), bf16[4,128,256]{2,1,0:T(8,128)(2,1)S(1)}, u32[]{:S(2)}, u32[]{:S(2)}) async-start(bf16[4,128,256]{2,1,0:T(8,128)(2,1)} %broadcast_in_dim.13), calls=%async_computation.1 | async-start | bytes 524288 | tf_op jit(solution)/shard_map/all_to_all | solution.py:167
  8.6 20.1 %copy-start = (bf16[2,1,128,1024]{3,2,1,0:T(8,128)(2,1)S(1)}, bf16[2,1,128,1024]{3,2,1,0:T(8,128)(2,1)}, u32[]{:S(2)}) copy-start(bf16[2,1,128,1024]{3,2,1,0:T(8,128)(2,1)} %q_ref.3) | copy-start | bytes 1572868
  8.6 4.4 %collective-permute-start = (bf16[128,256]{1,0:T(8,128)(2,1)S(1)}, bf16[128,256]{1,0:T(8,128)(2,1)S(1)}, u32[]{:S(2)}, u32[]{:S(2)}) collective-permute-start(bf16[128,256]{1,0:T(8,128)(2,1)S(1)} %get-tuple-element.20), channel_id=1, source_target_pairs={{0,24},{8,0},{16,8},{24,16},{1,25},{9,1},{17,9},{25,17},{2,26},{10... | collective-permute-start | bytes 196616 | tf_op jit(solution)/shard_map/ppermute | solution.py:190
  18.3 10.4 %all-to-all-start = ((bf16[4,128,256]{2,1,0:T(8,128)(2,1)}), bf16[4,128,256]{2,1,0:T(8,128)(2,1)S(1)}, u32[]{:S(2)}, u32[]{:S(2)}) async-start(bf16[4,128,256]{2,1,0:T(8,128)(2,1)} %broadcast_in_dim.12), calls=%async_computation | async-start | bytes 524288 | tf_op jit(solution)/shard_map/all_to_all | solution.py:167
  21.7 7.0 %copy-start.2 = (s32[8]{0:T(128)S(1)}, s32[8]{0:T(128)}, u32[]{:S(2)}) copy-start(s32[8]{0:T(128)} %order_ref.3) | copy-start | bytes 100
  21.7 7.0 %collective-permute-start.2 = (bf16[512,256]{1,0:T(8,128)(2,1)S(1)}, bf16[512,256]{1,0:T(8,128)(2,1)S(1)}, u32[]{:S(2)}, u32[]{:S(2)}) collective-permute-start(bf16[512,256]{1,0:T(8,128)(2,1)S(1)} %bitcast.20), channel_id=1, source_target_pairs={{0,1},{1,0},{2,3},{3,2},{4,5},{5,4},{6,7},{7,6},{8,9},{9,8},{10,11... | collective-permute-start | bytes 786440 | tf_op jit(solution)/shard_map/ppermute | solution.py:163
  28.7 6.4 %collective-permute-start.1 = (bf16[512,256]{1,0:T(8,128)(2,1)S(1)}, bf16[512,256]{1,0:T(8,128)(2,1)S(1)}, u32[]{:S(2)}, u32[]{:S(2)}) collective-permute-start(bf16[512,256]{1,0:T(8,128)(2,1)S(1)} %bitcast.22), channel_id=1, source_target_pairs={{0,1},{1,0},{2,3},{3,2},{4,5},{5,4},{6,7},{7,6},{8,9},{9,8},{10,11... | collective-permute-start | bytes 786440 | tf_op jit(solution)/shard_map/ppermute | solution.py:163
  34.5 6.3 %collective-permute-start.3 = (bf16[512,256]{1,0:T(8,128)(2,1)S(1)}, bf16[512,256]{1,0:T(8,128)(2,1)S(1)}, u32[]{:S(2)}, u32[]{:S(2)}) collective-permute-start(bf16[512,256]{1,0:T(8,128)(2,1)S(1)} %get-tuple-element.12), channel_id=1, source_target_pairs={{0,1},{1,0},{2,3},{3,2},{4,5},{5,4},{6,7},{7,6},{8,9},{9,8},{10,11... | collective-permute-start | bytes 786440 | tf_op jit(solution)/shard_map/ppermute | solution.py:163
  40.9 4.2 %collective-permute-start.5 = (bf16[512,256]{1,0:T(8,128)(2,1)S(1)}, bf16[512,256]{1,0:T(8,128)(2,1)S(1)}, u32[]{:S(2)}, u32[]{:S(2)}) collective-permute-start(bf16[512,256]{1,0:T(8,128)(2,1)S(1)} %get-tuple-element.14), channel_id=1, source_target_pairs={{0,1},{1,0},{2,3},{3,2},{4,5},{5,4},{6,7},{7,6},{8,9},{9,8},{10,11... | collective-permute-start | bytes 786440 | tf_op jit(solution)/shard_map/ppermute | solution.py:163
  41.6 13.2 %all-to-all-start.2 = ((bf16[4,128,256]{2,1,0:T(8,128)(2,1)}), bf16[4,128,256]{2,1,0:T(8,128)(2,1)S(1)}, u32[]{:S(2)}, u32[]{:S(2)}) async-start(bf16[4,128,256]{2,1,0:T(8,128)(2,1)} %bitcast.6), calls=%async_computation.2 | async-start | bytes 524288 | tf_op jit(solution)/shard_map/all_to_all | solution.py:167
  54.8 11.6 %all-to-all-start.3 = ((bf16[4,128,256]{2,1,0:T(8,128)(2,1)}), bf16[4,128,256]{2,1,0:T(8,128)(2,1)S(1)}, u32[]{:S(2)}, u32[]{:S(2)}) async-start(bf16[4,128,256]{2,1,0:T(8,128)(2,1)} %bitcast.8), calls=%async_computation.3 | async-start | bytes 524288 | tf_op jit(solution)/shard_map/all_to_all | solution.py:167
  58.2 0.8 %copy-start.3 = (f32[1,128,128]{2,1,0:T(8,128)S(1)}, f32[1,128,128]{2,1,0:T(8,128)}, u32[]{:S(2)}) copy-start(f32[1,128,128]{2,1,0:T(8,128)} %param.16) | copy-start | bytes 196612
  58.3 0.9 %copy-start.4 = (f32[1,128,128]{2,1,0:T(8,128)S(1)}, f32[1,128,128]{2,1,0:T(8,128)}, u32[]{:S(2)}) copy-start(f32[1,128,128]{2,1,0:T(8,128)} %param.15) | copy-start | bytes 196612
  59.1 7.3 %collective-permute-start.4 = (f32[128,256]{1,0:T(8,128)S(1)}, f32[128,256]{1,0:T(8,128)S(1)}, u32[]{:S(2)}, u32[]{:S(2)}) collective-permute-start(f32[128,256]{1,0:T(8,128)S(1)} %maximum_add_fusion), channel_id=1, source_target_pairs={{8,0},{16,8},{24,16},{9,1},{17,9},{25,17},{10,2},{18,10},{26,18},{... | collective-permute-start | bytes 393224 | tf_op jit(solution)/shard_map/ppermute | solution.py:210
